TPU v7x, 256 devices: a whole 4x4x8 slice. The times are simulated.
256 devices in a mesh: tm: 8 (over z), space: 32 (over y, x, core).
Axes of the slice: x: 4, y: 4, z: 8, core: 2. Of those that a mesh axis runs over, the one named last changes fastest.
Arguments:
- latent: bfloat16 [8, 64, 160, 384], P('tm', 'space'), may hold values from -6 to 6
- attn_gain: float32 [384], replicated, may hold values from 0.85 to 4.2
- qkv_weight: bfloat16 [384, 1152], replicated, may hold values from -1.5 to 1.5
- proj_weight: bfloat16 [384, 384], replicated, may hold values from -0.625 to 0.625
- conv_gain: float32 [384], replicated, may hold values from 0.25 to 1.75
- conv_weight: bfloat16 [3, 3, 3, 384, 384], replicated, may hold values from -0.0625 to 0.0625
- conv_bias: float32 [384], replicated, may hold values from -1.2 to 1.2
- time_weight: bfloat16 [3, 384, 768], replicated, may hold values from -0.1875 to 0.1875
- time_bias: float32 [768], replicated, may hold values from -1.2 to 1.2
- up_weight: bfloat16 [3, 3, 384, 192], replicated, may hold values from -0.109375 to 0.109375
- up_bias: float32 [192], replicated, may hold values from -1.2 to 1.2
Outputs:
- video: bfloat16 [16, 128, 320, 192], P('tm', 'space')
All inputs are finite; a program needn't handle non-finite values.
Results may differ from a plain program's by a relative error of at most 0.015.
Values may be sent and summed in bfloat16 or wider, within the bound.
A program may use at most 128 MiB of HBM per device.

v0:
```python
import math

import jax
import jax.numpy as jnp
from jax import lax
from jax.experimental import pallas as pl
from jax.experimental.pallas import tpu as pltpu
from jax.sharding import PartitionSpec as P

MESH = pl.DeviceIdType.MESH
F32 = jnp.float32
BF16 = jnp.bfloat16
C = 384
COLS = 160
NT = (((1,), (1,)), ((), ()))


def rms(x, gain):
    values = x.astype(F32)
    return values * lax.rsqrt(jnp.mean(values * values, axis=-1, keepdims=True) + 1e-06) * gain


def silu(x):
    return x / (1.0 + jnp.exp(-x))


def dot(a, b):
    return jnp.dot(a, b, preferred_element_type=F32)


def flat(x):
    return x.reshape(-1, x.shape[-1])


def moved(x, steps):
    index = lax.broadcasted_iota(jnp.int32, x.shape, 0)
    edge = 0 if steps == 1 else COLS - 1
    rolled = pltpu.roll(x, steps % x.shape[0], 0)
    keep = index != edge
    for run in range(1, x.shape[0] // COLS):
        keep = keep & (index != edge + run * COLS)
    return jnp.where(keep, rolled, 0.0)


def kernel(
    latent, attn_gain, qkv_hbm, proj_hbm, conv_gain, conv_hbm, conv_bias, time_hbm, time_bias, up_hbm, up_bias,
    out,
    lat, nb, qb, acc, mx, den, acc_in, mx_in, den_in,
    qkv, proj, wc, wt, wu,
    mid, mid_in, act, conv, blocks, frames, wide,
    ss, rs, ws,
):
    z = lax.axis_index("tm")
    s = lax.axis_index("space")
    core = lax.rem(s, 2)
    x = lax.rem(s // 2, 4)
    y = s // 8
    pos1 = x + core * (y - x)
    pos2 = y + core * (x - y)
    step1 = 2 + 6 * core
    step2 = 8 - 6 * core

    def at(zz, ss_):
        return (zz, ss_)

    sib = at(z, s + 1 - 2 * core)
    far = at(z, lax.rem(s + 2 * core + 31, 32))
    f_plus = at(z, s + (lax.rem(pos1 + 1, 4) - pos1) * step1)
    f_minus = at(z, s + (lax.rem(pos1 + 3, 4) - pos1) * step1)
    g_plus = at(z, s + (lax.rem(pos2 + 1, 4) - pos2) * step2)
    g_minus = at(z, s + (lax.rem(pos2 + 3, 4) - pos2) * step2)
    z_plus = at(lax.rem(z + 1, 8), s)
    z_minus = at(lax.rem(z + 7, 8), s)
    z_plus2 = at(lax.rem(z + 2, 8), s)
    z_minus2 = at(lax.rem(z + 6, 8), s)
    s_up = at(z, lax.rem(s + 31, 32))
    s_down = at(z, lax.rem(s + 1, 32))

    pending = []
    local = []

    def send(src, dst, device):
        k = len(pending)
        copy = pltpu.make_async_remote_copy(
            src_ref=src, dst_ref=dst, send_sem=ss.at[k], recv_sem=rs.at[k], device_id=device, device_id_type=MESH
        )
        copy.start()
        pending.append(copy)
        return copy

    def load(src, dst):
        copy = pltpu.make_async_copy(src, dst, ws.at[len(local)])
        copy.start()
        local.append(copy)
        return copy

    barrier = pltpu.get_barrier_semaphore()
    partners = (sib, far, f_plus, f_minus, g_plus, g_minus, z_plus, z_minus, z_plus2, z_minus2)
    for partner in partners:
        pl.semaphore_signal(barrier, inc=1, device_id=partner, device_id_type=MESH)
    qkv_load = load(qkv_hbm, qkv)
    pl.semaphore_wait(barrier, len(partners))

    shift = [send(latent.at[0, r], lat.at[r], z_plus2) for r in range(2)]
    proj_load = load(proj_hbm, proj)
    conv_loads = [
        [load(conv_hbm.at[dt, :, dx], wc.at[dt, :, :, pl.ds(dx * C, C)]) for dx in range(3)] for dt in range(3)
    ]
    time_load = load(time_hbm, wt)
    up_load = load(up_hbm, wu)

    mx[...] = jnp.full(mx.shape, -1e30, F32)
    den[...] = jnp.zeros(den.shape, F32)
    acc[...] = jnp.zeros(acc.shape, F32)

    fp, fm, op, g, go = {}, {}, {}, {}, {}

    def along_second(r, i):
        g[r, i] = (send(nb.at[r, 0, i], nb.at[r, 3, i], g_plus), send(nb.at[r, 0, i], nb.at[r, 1, i], g_minus))

    def own(r):
        shift[r].wait_recv()
        nb[r, 0, 0] = rms(lat[r], attn_gain[...]).astype(BF16)
        fp[r] = send(nb.at[r, 0, 0], nb.at[r, 0, 3], f_plus)
        fm[r] = send(nb.at[r, 0, 0], nb.at[r, 0, 1], f_minus)
        along_second(r, 0)

    def first_axis(r):
        fp[r].wait_recv()
        if r == 0:
            op[r] = send(nb.at[r, 0, 3], nb.at[r, 0, 2], f_plus)
        along_second(r, 3)
        fm[r].wait_recv()
        if r == 1:
            op[r] = send(nb.at[r, 0, 1], nb.at[r, 0, 2], f_minus)
        along_second(r, 1)
        op[r].wait_recv()
        along_second(r, 2)

    def second_axis(r):
        for i in (0, 3, 1, 2):
            plus, minus = g[r, i]
            plus.wait_recv()
            if (r + i) % 2 == 0:
                go[r, i] = send(nb.at[r, 3, i], nb.at[r, 2, i], g_plus)
            minus.wait_recv()
            if (r + i) % 2 == 1:
                go[r, i] = send(nb.at[r, 1, i], nb.at[r, 2, i], g_minus)

    def last(r):
        for i in (0, 3, 1, 2):
            go[r, i].wait_recv()

    def attend(r, j, tiles=(0, 4)):
        def tile(t, carry):
            keys = flat(nb[r, j])
            scores = lax.dot_general(qb[t], keys, NT, preferred_element_type=F32)
            top = mx[t]
            new_top = jnp.maximum(top, jnp.max(scores, axis=1, keepdims=True))
            expo = jnp.exp2(scores - new_top[:, :1])
            fade = jnp.exp2(top - new_top)
            mx[t] = new_top
            den[t] = den[t] * fade + jnp.sum(expo, axis=1, keepdims=True)
            acc[t] = acc[t] * fade[:, :1] + dot(expo.astype(BF16), keys)
            return carry

        lax.fori_loop(tiles[0], tiles[1], tile, 0)

    own(0)
    first_axis(0)
    own(1)
    qkv_load.wait()
    scale = math.log2(math.e) / math.sqrt(C)
    normed = jnp.concatenate([nb[0, 0, 0], nb[1, 0, 0]], axis=0)
    query = dot(normed, qkv[:, :C]).astype(BF16)
    query = lax.dot_general(query, qkv[:, C : 2 * C], NT, preferred_element_type=F32) * scale
    qb[0:2] = query.astype(BF16).reshape(2, COLS, C)
    q_copy = send(qb.at[0:2], qb.at[2:4], sib)
    second_axis(0)
    first_axis(1)
    q_copy.wait_recv()
    attend(0, 0)
    attend(0, 3)
    attend(0, 1)
    second_axis(1)
    last(0)
    attend(0, 2)
    attend(1, 0)
    attend(1, 3)
    attend(1, 1)
    last(1)
    attend(1, 2, (2, 4))
    back = [
        send(acc.at[2:4], acc_in, sib),
        send(mx.at[2:4], mx_in, sib),
        send(den.at[2:4], den_in, sib),
    ]
    attend(1, 2, (0, 2))
    proj_load.wait()
    for copy in back:
        copy.wait_recv()
    top = jnp.maximum(mx[0:2], mx_in[...])
    mine = jnp.exp2(mx[0:2] - top)
    other = jnp.exp2(mx_in[...] - top)
    total = den[0:2] * mine + den_in[...] * other
    mine = (mine / total)[:, :, :1]
    other = (other / total)[:, :, :1]
    pooled = flat(acc[0:2] * mine + acc_in[...] * other).astype(BF16)
    attn = dot(pooled, qkv[:, 2 * C :]).astype(BF16)
    value = (flat(lat[...]).astype(F32) + dot(attn, proj[...])).astype(BF16)
    mid[...] = value.reshape(2, COLS, C)
    act[1, 1:3] = silu(rms(value, conv_gain[...])).astype(BF16).reshape(2, COLS, C)

    to_next = send(act.at[1, 1:3], act.at[0, 1:3], z_plus)
    to_previous = send(mid, mid_in, z_minus)

    def edges(f):
        return [send(act.at[f, 1], act.at[f, 3], s_up), send(act.at[f, 2], act.at[f, 0], s_down)]

    def settle(copies, f):
        for copy in copies:
            copy.wait_recv()

        @pl.when(s == 0)
        def _():
            act[f, 0] = jnp.zeros((COLS, C), BF16)

        @pl.when(s == 31)
        def _():
            act[f, 3] = jnp.zeros((COLS, C), BF16)

    def convolve(f):
        taps = jnp.concatenate([flat(act[f, dy : dy + 2]) for dy in range(3)], axis=1)
        conv[...] += dot(taps, wc[f].reshape(3 * C, 3 * C))

    halo = {1: edges(1)}
    conv[...] = jnp.zeros(conv.shape, F32)
    for row in conv_loads:
        for copy in row:
            copy.wait()
    settle(halo[1], 1)

    @pl.when(z != 1)
    def _():
        convolve(1)

    to_next.wait_recv()
    halo[0] = edges(0)
    to_previous.wait_recv()
    act[2, 1:3] = silu(rms(flat(mid_in[...]), conv_gain[...])).astype(BF16).reshape(2, COLS, C)
    halo[2] = edges(2)
    settle(halo[0], 0)

    @pl.when((z != 1) & (z != 2))
    def _():
        convolve(0)

    settle(halo[2], 2)
    convolve(2)
    value = conv[:, C : 2 * C] + moved(conv[:, :C], 1) + moved(conv[:, 2 * C :], -1)
    value = (value + conv_bias[...] + flat(mid_in[...]).astype(F32)).astype(BF16)
    blocks[1] = value
    next_block = send(blocks.at[1], blocks.at[0], z_plus)
    previous_block = send(blocks.at[1], blocks.at[2], z_minus)
    time_load.wait()
    total = dot(jnp.where(z >= 1, value, jnp.zeros_like(value)), wt[1]) + time_bias[...]
    next_block.wait_recv()
    total += dot(jnp.where(z >= 2, blocks[0], jnp.zeros_like(value)), wt[0])
    previous_block.wait_recv()
    total += dot(blocks[2], wt[2])
    doubled = total.astype(BF16).reshape(2, COLS, 2 * C)
    frames[1:3, 0] = doubled[:, :, :C]
    frames[1:3, 1] = doubled[:, :, C:]
    above = send(frames.at[1], frames.at[3], s_up)
    below = send(frames.at[2], frames.at[0], s_down)
    up_load.wait()

    def upsample(i, a):
        taps = jnp.concatenate([flat(frames[i + a]), flat(frames[i + a + 1])], axis=1)
        value = dot(taps, wu[a])
        side = value[:, C:]
        lane = lax.broadcasted_iota(jnp.int32, side.shape, 1)
        value = value[:, :C] + jnp.where(lane < C // 2, moved(side, 1), moved(side, -1)) + up_bias[...]
        second = pltpu.roll(value, C // 2, 1)
        for frame in range(2):
            rows = slice(frame * COLS, (frame + 1) * COLS)
            for part in range(2):
                lanes = slice(128 * part, 128 * part + 128)
                wide[part, pl.ds(0, COLS, stride=2), :] = value[rows, lanes]
                wide[part, pl.ds(1, COLS, stride=2), :] = second[rows, lanes]
            out[frame, 2 * i + a, :, :128] = wide[0].astype(BF16)
            out[frame, 2 * i + a, :, 128:] = wide[1, :, : C // 2 - 128].astype(BF16)

    upsample(0, 1)
    upsample(1, 0)
    above.wait_recv()
    below.wait_recv()

    @pl.when(s == 0)
    def _():
        frames[0] = jnp.zeros((2, COLS, C), BF16)

    @pl.when(s == 31)
    def _():
        frames[3] = jnp.zeros((2, COLS, C), BF16)

    upsample(0, 0)
    upsample(1, 1)
    for copy in pending:
        copy.wait_send()


def up_table(up_weight):
    weight = up_weight.astype(F32)
    rows = [[weight[0], weight[1] + weight[2]], [weight[0] + weight[1], weight[2]]]

    def cell(a, b, e, f):
        row = rows[a][e]
        return [[row[0], row[1] + row[2]], [row[0] + row[1], row[2]]][b][f].astype(BF16)

    return jnp.stack(
        [
            jnp.concatenate(
                [
                    jnp.concatenate([cell(a, b, e, f) for b, f in ((0, 1), (1, 0), (0, 0), (1, 1))], axis=1)
                    for e in range(2)
                ],
                axis=0,
            )
            for a in range(2)
        ]
    )


SENDS = 64
LOADS = 16


def body(
    latent, attn_gain, qkv_weight, proj_weight, conv_gain, conv_weight, conv_bias, time_weight, time_bias, up_weight,
    up_bias,
):
    table = up_table(up_weight)
    bias2 = jnp.concatenate([up_bias, up_bias])
    vmem = pl.BlockSpec(memory_space=pltpu.VMEM)
    anywhere = pl.BlockSpec(memory_space=pl.ANY)
    return pl.pallas_call(
        kernel,
        out_shape=jax.ShapeDtypeStruct((2, 4, 2 * COLS, C // 2), BF16),
        in_specs=[
            anywhere, vmem, anywhere, anywhere, vmem, anywhere, vmem, anywhere, vmem, anywhere, vmem,
        ],
        out_specs=vmem,
        scratch_shapes=[
            pltpu.VMEM((2, COLS, C), BF16),
            pltpu.VMEM((2, 4, 4, COLS, C), BF16),
            pltpu.VMEM((4, COLS, C), BF16),
            pltpu.VMEM((4, COLS, C), F32),
            pltpu.VMEM((4, COLS, 128), F32),
            pltpu.VMEM((4, COLS, 128), F32),
            pltpu.VMEM((2, COLS, C), F32),
            pltpu.VMEM((2, COLS, 128), F32),
            pltpu.VMEM((2, COLS, 128), F32),
            pltpu.VMEM((C, 3 * C), BF16),
            pltpu.VMEM((C, C), BF16),
            pltpu.VMEM((3, 3, C, 3 * C), BF16),
            pltpu.VMEM((3, C, 2 * C), BF16),
            pltpu.VMEM((2, 2 * C, 2 * C), BF16),
            pltpu.VMEM((2, COLS, C), BF16),
            pltpu.VMEM((2, COLS, C), BF16),
            pltpu.VMEM((3, 4, COLS, C), BF16),
            pltpu.VMEM((2 * COLS, 3 * C), F32),
            pltpu.VMEM((3, 2 * COLS, C), BF16),
            pltpu.VMEM((4, 2, COLS, C), BF16),
            pltpu.VMEM((2, 2 * COLS, 128), F32),
            pltpu.SemaphoreType.DMA((SENDS,)),
            pltpu.SemaphoreType.DMA((SENDS,)),
            pltpu.SemaphoreType.DMA((LOADS,)),
        ],
        compiler_params=pltpu.CompilerParams(
            collective_id=0, has_side_effects=True, vmem_limit_bytes=56 * 1024 * 1024
        ),
    )(
        latent, attn_gain[None], qkv_weight, proj_weight, conv_gain[None], conv_weight, conv_bias[None], time_weight,
        time_bias[None], table, bias2[None],
    )


def solution(mesh):
    return jax.shard_map(
        body,
        mesh=mesh,
        in_specs=(P("tm", "space", None, None), P(), P(), P(), P(), P(), P(), P(), P(), P(), P()),
        out_specs=P("tm", "space", None, None),
        check_vma=False,
    )
```

profile of v0, /device:TPU:1, one launch (start us, length us, event | category | flops | bytes accessed | tf_op | source)
XLA Modules:
  0.0 114.1 jit_solution(2327921006699489920)
XLA Ops:
  0.0 2.5 %copy.12 = bf16[3,3,384,192]{3,2,1,0:T(8,128)(2,1)S(1)} copy(bf16[3,3,384,192]{2,3,1,0:T(8,128)(2,1)} %param.20) | data formatting | bytes 2654208 | tf_op args[9]
  2.5 0.3 convert_element_type.107
  2.9 0.3 slice_add_fusion.1
  3.2 0.1 fusion.10
  3.4 0.1 fusion.12
  3.5 0.1 fusion.1
  3.6 0.2 fusion.8
  3.8 7.8 %maximum_bitcast_fusion = (bf16[1,768,768]{2,1,0:T(8,128)(2,1)S(1)}, bf16[1,768,768]{2,1,0:T(8,128)(2,1)S(1)}) fusion(bf16[384,192]{1,0:T(8,128)(2,1)S(1)} %get-tuple-element.18, bf16[384,192]{1,0:T(8,128)(2,1)S(1)} %get-tuple-element.17, bf16[384,192]{1,0:T(8,128)(2,1)S(1)} %get-tuple-element.16, bf16[384,192]{1,0:T(8,128)(2,1)S(1)} %get-tuple-element.15, ...), kind=kLoop, calls=%fused_computation.3 | loop fusion | flops 18874368 | bytes 4718592 | tf_op jit(solution)/shard_map/stack | solution.py:321
  11.6 0.0 copy-start.4
  11.6 0.0 copy-start
  11.6 0.0 copy-start.1
  11.6 0.0 copy-start.2
  11.6 0.0 copy-start.3
  11.6 1.6 %pad_maximum_fusion.up_hbm = bf16[2,768,768]{2,1,0:T(8,128)(2,1)} fusion(bf16[1,768,768]{2,1,0:T(8,128)(2,1)S(1)} %get-tuple-element.24, bf16[1,768,768]{2,1,0:T(8,128)(2,1)S(1)} %get-tuple-element.23), kind=kLoop, calls=%fused_computation | loop fusion | flops 1179648 | bytes 4718592 | tf_op jit(solution)/shard_map/stack | solution.py:321
  13.3 0.0 copy-done.4
  13.3 0.1 pad_maximum_fusion.1
  13.3 0.6 broadcast_in_dim.19.up_bias
  13.9 0.0 copy-done
  13.9 0.6 broadcast_in_dim.18.time_bias
  14.5 0.0 copy-done.1
  14.5 0.6 broadcast_in_dim.15.attn_gain
  15.1 0.0 copy-done.2
  15.1 0.6 broadcast_in_dim.16.conv_gain
  15.7 0.0 copy-done.3
  15.7 0.6 broadcast_in_dim.17.conv_bias
  16.3 95.3 %shard_map.109 = bf16[2,4,320,192]{3,2,1,0:T(8,128)(2,1)} custom-call(bf16[1,2,160,384]{3,2,1,0:T(8,128)(2,1)} %latent.1, f32[1,384]{1,0:T(1,128)} %broadcast_in_dim.15.attn_gain, bf16[384,1152]{1,0:T(8,128)(2,1)} %qkv_hbm.1, bf16[384,384]{1,0:T(8,128)(2,1)} %proj_hbm.1, f32[1,384]{1,0:T(1,128)} %broadcast_in_dim.16.conv_gain, ...), custom_call_target="tpu_custom_call" | custom-call | tf_op jit(solution)/shard_map/pallas_call | solution.py:347
  111.6 2.5 %copy.13 = bf16[2,4,320,192]{2,3,1,0:T(8,128)(2,1)} copy(bf16[2,4,320,192]{3,2,1,0:T(8,128)(2,1)} %shard_map.109) | data formatting | bytes 1966080 | tf_op jit(solution)/shard_map/pallas_call | solution.py:347
  (2 shorter events, 0.1 us)
Async XLA Ops:
  11.6 1.7 %copy-start.4 = (f32[192]{0:T(256)S(1)}, f32[192]{0:T(256)}, u32[]{:S(2)}) copy-start(f32[192]{0:T(256)} %param.21) | copy-start | bytes 2308
  11.6 2.3 %copy-start = (f32[768]{0:T(1024)S(1)}, f32[768]{0:T(1024)}, u32[]{:S(2)}) copy-start(f32[768]{0:T(1024)} %param.19) | copy-start | bytes 9220
  11.6 2.9 %copy-start.1 = (f32[384]{0:T(512)S(1)}, f32[384]{0:T(512)}, u32[]{:S(2)}) copy-start(f32[384]{0:T(512)} %param.12) | copy-start | bytes 4612
  11.6 3.5 %copy-start.2 = (f32[384]{0:T(512)S(1)}, f32[384]{0:T(512)}, u32[]{:S(2)}) copy-start(f32[384]{0:T(512)} %param.15) | copy-start | bytes 4612
  11.6 4.1 %copy-start.3 = (f32[384]{0:T(512)S(1)}, f32[384]{0:T(512)}, u32[]{:S(2)}) copy-start(f32[384]{0:T(512)} %param.17) | copy-start | bytes 4612
where the time goes:
time: 115 us; the launch traced here: 114 us
  Pallas kernels  95.3 us (83%)
  other arithmetic  10.5 us (9%)
  local copies, waits for them, and re-layouts  8.1 us (7%)
    pallas_call x1, Pallas kernels, body(): pl.pallas_call(kernel, out_shape=jax.ShapeDtypeStruct((2, 4, 2 * COLS, C...  95.3 us
    another operation x2, other arithmetic, up_table(): jnp.stack([jnp.concatenate([jnp.concatenate([cell(a, b, e, f) for b, f in...  9.42 us
    unnamed x11, local copies, waits for them, and re-layouts  2.55 us
    pallas_call x1, local copies, waits for them, and re-layouts, body(): pl.pallas_call(kernel, out_shape=jax.ShapeDtypeStruct((2, 4, 2 * COLS, C...  2.47 us

commit v1 on v0

v1 whole, which is shorter than its diff:
```python
import math

import jax
import jax.numpy as jnp
from jax import lax
from jax.experimental import pallas as pl
from jax.experimental.pallas import tpu as pltpu
from jax.sharding import PartitionSpec as P

MESH = pl.DeviceIdType.MESH
F32 = jnp.float32
BF16 = jnp.bfloat16
C = 384
COLS = 160
NT = (((1,), (1,)), ((), ()))
PARTS = 4
PART = 80
OWN = PARTS * PART
SIDES = (0, 3, 1, 2)
ORDER = (
    ("own", 0), ("own", 1), ("f+", 0), ("f-", 0), ("g+", 0, 0), ("g-", 0, 0), ("own", 2), ("f-", 1), ("g-", 1, 0),
    ("g-", 0, 3), ("g-", 0, 1), ("f+", 1), ("g+", 1, 0), ("own", 3), ("f-", 2), ("g-", 2, 0), ("g+", 0, 3),
    ("op", 0), ("g+", 0, 1), ("go", 0, 0), ("query", 0), ("f+", 2), ("g+", 2, 0), ("attend", 0, 0, 1), ("g+", 1, 1),
    ("g-", 1, 1), ("op", 1), ("g+", 1, 3), ("go", 1, 0), ("go", 0, 3), ("go", 0, 1), ("f+", 3), ("g+", 3, 0),
    ("g+", 2, 1), ("g+", 0, 2), ("g-", 1, 3), ("f-", 3), ("g-", 3, 0), ("g-", 2, 1), ("g-", 0, 2),
    ("attend", 0, 1, 2), ("table", 0), ("g-", 2, 3), ("g-", 1, 2), ("g+", 2, 3), ("op", 2), ("go", 2, 0),
    ("g-", 3, 3), ("go", 1, 1), ("g+", 1, 2), ("attend", 1, 1, 2), ("go", 1, 3), ("g+", 3, 3), ("go", 0, 2),
    ("g+", 3, 1), ("g+", 2, 2), ("g-", 3, 1), ("op", 3), ("go", 3, 0), ("go", 2, 1), ("attend", 0, 3, 2),
    ("go", 2, 3), ("go", 1, 2), ("g-", 2, 2), ("attend", 1, 3, 2), ("g-", 3, 2), ("attend", 2, 1, 2), ("go", 3, 3),
    ("go", 3, 1), ("go", 2, 2), ("g+", 3, 2), ("attend", 2, 3, 2), ("go", 3, 2), ("attend", 3, 1, 2),
)


def rms(x, gain):
    values = x.astype(F32)
    return values * lax.rsqrt(jnp.mean(values * values, axis=-1, keepdims=True) + 1e-06) * gain


def silu(x):
    return x / (1.0 + jnp.exp(-x))


def dot(a, b):
    return jnp.dot(a, b, preferred_element_type=F32)


def flat(x):
    return x.reshape(-1, x.shape[-1])


def moved(x, steps):
    index = lax.broadcasted_iota(jnp.int32, x.shape, 0)
    edge = 0 if steps == 1 else COLS - 1
    rolled = pltpu.roll(x, steps % x.shape[0], 0)
    keep = index != edge
    for run in range(1, x.shape[0] // COLS):
        keep = keep & (index != edge + run * COLS)
    return jnp.where(keep, rolled, 0.0)


def kernel(
    latent, attn_gain, qkv_hbm, proj_hbm, conv_gain, conv_hbm, conv_bias, time_hbm, time_bias, up_hbm, up_bias,
    out,
    lat, nb, qb, acc, mx, den, acc_in, mx_in, den_in,
    qkv, proj, wc, wt, up, wu,
    mid, mid_in, act, conv, blocks, frames, wide,
    ss, rs, ws,
):
    z = lax.axis_index("tm")
    s = lax.axis_index("space")
    core = lax.rem(s, 2)
    x = lax.rem(s // 2, 4)
    y = s // 8
    pos1 = x + core * (y - x)
    pos2 = y + core * (x - y)
    step1 = 2 + 6 * core
    step2 = 8 - 6 * core

    def at(zz, ss_):
        return (zz, ss_)

    sib = at(z, s + 1 - 2 * core)
    far = at(z, lax.rem(s + 2 * core + 31, 32))
    f_plus = at(z, s + (lax.rem(pos1 + 1, 4) - pos1) * step1)
    f_minus = at(z, s + (lax.rem(pos1 + 3, 4) - pos1) * step1)
    g_plus = at(z, s + (lax.rem(pos2 + 1, 4) - pos2) * step2)
    g_minus = at(z, s + (lax.rem(pos2 + 3, 4) - pos2) * step2)
    z_plus = at(lax.rem(z + 1, 8), s)
    z_minus = at(lax.rem(z + 7, 8), s)
    z_plus2 = at(lax.rem(z + 2, 8), s)
    z_minus2 = at(lax.rem(z + 6, 8), s)
    s_up = at(z, lax.rem(s + 31, 32))
    s_down = at(z, lax.rem(s + 1, 32))

    pending = []
    local = []

    def send(src, dst, device):
        k = len(pending)
        copy = pltpu.make_async_remote_copy(
            src_ref=src, dst_ref=dst, send_sem=ss.at[k], recv_sem=rs.at[k], device_id=device, device_id_type=MESH
        )
        copy.start()
        pending.append(copy)
        return copy


    def load(src, dst):
        copy = pltpu.make_async_copy(src, dst, ws.at[len(local)])
        copy.start()
        local.append(copy)
        return copy

    barrier = pltpu.get_barrier_semaphore()
    partners = (sib, far, f_plus, f_minus, g_plus, g_minus, z_plus, z_minus, z_plus2, z_minus2)
    for partner in partners:
        pl.semaphore_signal(barrier, inc=1, device_id=partner, device_id_type=MESH)
    qkv_load = load(qkv_hbm, qkv)
    pl.semaphore_wait(barrier, len(partners))

    shift = [
        send(latent.at[0, c // 2, pl.ds(c % 2 * PART, PART)], lat.at[c], z_plus2) for c in range(PARTS)
    ]
    proj_load = load(proj_hbm, proj)
    conv_loads = [
        [load(conv_hbm.at[dt, :, dx], wc.at[dt, :, :, pl.ds(dx * C, C)]) for dx in range(3)] for dt in range(3)
    ]
    time_load = load(time_hbm, wt)
    up_load = load(up_hbm, up)

    mx[...] = jnp.full(mx.shape, -1e30, F32)
    den[...] = jnp.zeros(den.shape, F32)
    acc[...] = jnp.zeros(acc.shape, F32)

    copies = {}

    def slot(c, j, i):
        return nb.at[4 * c + SIDES.index(j), i]

    def along_second(c, i):
        copies["g+", c, i] = send(slot(c, 0, i), slot(c, 3, i), g_plus)
        copies["g-", c, i] = send(slot(c, 0, i), slot(c, 1, i), g_minus)

    def step(kind, c, i=0):
        if kind == "own":
            shift[c].wait_recv()
            nb[4 * c, 0] = rms(lat[c], attn_gain[...].reshape(1, C)).astype(BF16)
            copies["f+", c, 0] = send(slot(c, 0, 0), slot(c, 0, 3), f_plus)
            copies["f-", c, 0] = send(slot(c, 0, 0), slot(c, 0, 1), f_minus)
            along_second(c, 0)
            return
        copies[kind, c, i].wait_recv()
        if kind == "f+":
            if c % 2 == 0:
                copies["op", c, 0] = send(slot(c, 0, 3), slot(c, 0, 2), f_plus)
            along_second(c, 3)
        elif kind == "f-":
            if c % 2 == 1:
                copies["op", c, 0] = send(slot(c, 0, 1), slot(c, 0, 2), f_minus)
            along_second(c, 1)
        elif kind == "op":
            along_second(c, 2)
        elif kind == "g+" and (c + i) % 2 == 0:
            copies["go", c, i] = send(slot(c, 3, i), slot(c, 2, i), g_plus)
        elif kind == "g-" and (c + i) % 2 == 1:
            copies["go", c, i] = send(slot(c, 1, i), slot(c, 2, i), g_minus)

    def project():
        qkv_load.wait()
        scale = math.log2(math.e) / math.sqrt(C)
        normed = jnp.concatenate([nb[4 * c, 0] for c in range(PARTS)], axis=0)
        query = dot(normed, qkv[:, :C]).astype(BF16)
        query = lax.dot_general(query, qkv[:, C : 2 * C], NT, preferred_element_type=F32) * scale
        qb[:OWN] = query.astype(BF16)
        return send(qb.at[pl.ds(0, OWN)], qb.at[pl.ds(OWN, OWN)], sib)

    def attend(c, p, n, low=0, size=2 * OWN):
        rows = slice(low, low + size)
        count = n * OWN
        keys = nb[4 * c + p : 4 * c + p + n].reshape(count, C)
        scores = lax.dot_general(qb[rows], keys, NT, preferred_element_type=F32)
        top = mx[rows]
        new_top = jnp.maximum(top, jnp.max(scores, axis=1, keepdims=True))
        expo = jnp.exp2(scores - jnp.tile(new_top, (1, -(-count // 128)))[:, :count])
        fade = jnp.exp2(top - new_top)
        if count % 128 == 0:
            part = expo[:, :128]
            for lane in range(128, count, 128):
                part = part + expo[:, lane : lane + 128]
        else:
            part = jnp.sum(expo, axis=1, keepdims=True) * (1.0 / 128.0)
        mx[rows] = new_top
        den[rows] = den[rows] * fade + part
        acc[rows] = acc[rows] * jnp.tile(fade, (1, C // 128)) + dot(expo.astype(BF16), keys)

    def table():
        def summed(parts):
            return parts[0] if len(parts) == 1 else parts[0] + parts[1]

        spans = {(0, 0): (0,), (0, 1): (1, 2), (1, 0): (0, 1), (1, 1): (2,)}
        for a in range(2):
            for e in range(2):
                rows = [summed([up[dy, dx].astype(F32) for dy in spans[a, e]]) for dx in range(3)]
                for k, (b, f) in enumerate(((0, 1), (1, 0), (0, 0), (1, 1))):
                    cell = summed([rows[dx] for dx in spans[b, f]]).astype(BF16)
                    wu[a, k * C // 2 : (k + 1) * C // 2, e * C : (e + 1) * C] = cell

    for kind, c, *rest in ORDER:
        if kind == "query":
            q_copy = project()
        elif kind == "attend":
            attend(c, *rest)
        elif kind == "table":
            up_load.wait()
            table()
        else:
            step(kind, c, *rest)
            if (kind, c) == ("g+", 2) and rest == [0]:
                q_copy.wait_recv()
    attend(PARTS - 1, 3, 1, OWN, OWN)
    back = [
        send(acc.at[pl.ds(OWN, OWN)], acc_in, sib),
        send(mx.at[pl.ds(OWN, OWN)], mx_in, sib),
        send(den.at[pl.ds(OWN, OWN)], den_in, sib),
    ]
    attend(PARTS - 1, 3, 1, 0, OWN)
    proj_load.wait()
    for copy in back:
        copy.wait_recv()
    top = jnp.maximum(mx[:OWN], mx_in[...])
    mine = jnp.exp2(mx[:OWN] - top)
    other = jnp.exp2(mx_in[...] - top)
    total = jnp.sum(den[:OWN] * mine + den_in[...] * other, axis=1, keepdims=True)
    mine = jnp.tile(mine / total, (1, C // 128))
    other = jnp.tile(other / total, (1, C // 128))
    pooled = (acc[:OWN] * mine + acc_in[...] * other).astype(BF16)
    attn = dot(pooled, qkv[:, 2 * C :]).astype(BF16)
    value = (flat(lat[...]).astype(F32) + dot(attn, proj[...])).astype(BF16)
    mid[...] = value.reshape(2, COLS, C)
    act[1, 1:3] = silu(rms(value, conv_gain[...].reshape(1, C))).astype(BF16).reshape(2, COLS, C)


    to_next = send(act.at[1, 1:3], act.at[0, 1:3], z_plus)
    to_previous = send(mid, mid_in, z_minus)

    def edges(f):
        return [send(act.at[f, 1], act.at[f, 3], s_up), send(act.at[f, 2], act.at[f, 0], s_down)]

    def settle(copies, f):
        for copy in copies:
            copy.wait_recv()

        @pl.when(s == 0)
        def _():
            act[f, 0] = jnp.zeros((COLS, C), BF16)

        @pl.when(s == 31)
        def _():
            act[f, 3] = jnp.zeros((COLS, C), BF16)

    def convolve(f):
        taps = jnp.concatenate([flat(act[f, dy : dy + 2]) for dy in range(3)], axis=1)
        conv[...] += dot(taps, wc[f].reshape(3 * C, 3 * C))

    halo = {1: edges(1)}
    conv[...] = jnp.zeros(conv.shape, F32)
    for row in conv_loads:
        for copy in row:
            copy.wait()
    settle(halo[1], 1)

    @pl.when(z != 1)
    def _():
        convolve(1)

    to_next.wait_recv()
    halo[0] = edges(0)
    to_previous.wait_recv()
    act[2, 1:3] = silu(rms(flat(mid_in[...]), conv_gain[...].reshape(1, C))).astype(BF16).reshape(2, COLS, C)
    halo[2] = edges(2)
    settle(halo[0], 0)

    @pl.when((z != 1) & (z != 2))
    def _():
        convolve(0)

    settle(halo[2], 2)
    convolve(2)
    value = conv[:, C : 2 * C] + moved(conv[:, :C], 1) + moved(conv[:, 2 * C :], -1)
    value = (value + conv_bias[...].reshape(1, C) + flat(mid_in[...]).astype(F32)).astype(BF16)
    blocks[1] = value
    next_block = send(blocks.at[1], blocks.at[0], z_plus)
    previous_block = send(blocks.at[1], blocks.at[2], z_minus)
    time_load.wait()
    total = dot(jnp.where(z >= 1, value, jnp.zeros_like(value)), wt[1]) + time_bias[...].reshape(1, 2 * C)
    next_block.wait_recv()
    total += dot(jnp.where(z >= 2, blocks[0], jnp.zeros_like(value)), wt[0])
    previous_block.wait_recv()
    total += dot(blocks[2], wt[2])
    doubled = total.astype(BF16).reshape(2, COLS, 2 * C)
    frames[1:3, 0] = doubled[:, :, :C]
    frames[1:3, 1] = doubled[:, :, C:]
    above = send(frames.at[1], frames.at[3], s_up)
    below = send(frames.at[2], frames.at[0], s_down)

    bias = up_bias[...].reshape(1, C // 2)

    def upsample(i, a):
        taps = jnp.concatenate([flat(frames[i + a]), flat(frames[i + a + 1])], axis=1)
        value = lax.dot_general(taps, wu[a], NT, preferred_element_type=F32)
        side = value[:, C:]
        lane = lax.broadcasted_iota(jnp.int32, side.shape, 1)
        value = value[:, :C] + jnp.where(lane < C // 2, moved(side, 1), moved(side, -1))
        second = pltpu.roll(value, C // 2, 1)
        for frame in range(2):
            rows = slice(frame * COLS, (frame + 1) * COLS)
            for part in range(2):
                lanes = slice(128 * part, 128 * part + 128)
                wide[part, pl.ds(0, COLS, stride=2), :] = value[rows, lanes]
                wide[part, pl.ds(1, COLS, stride=2), :] = second[rows, lanes]
            out[frame, 2 * i + a, :, :128] = (wide[0] + bias[:, :128]).astype(BF16)
            out[frame, 2 * i + a, :, 128:] = (wide[1, :, : C // 2 - 128] + bias[:, 128:]).astype(BF16)

    upsample(0, 1)
    upsample(1, 0)
    above.wait_recv()
    below.wait_recv()

    @pl.when(s == 0)
    def _():
        frames[0] = jnp.zeros((2, COLS, C), BF16)

    @pl.when(s == 31)
    def _():
        frames[3] = jnp.zeros((2, COLS, C), BF16)

    upsample(0, 0)
    upsample(1, 1)
    for copy in pending:
        copy.wait_send()


SENDS = 96
LOADS = 16


def body(
    latent, attn_gain, qkv_weight, proj_weight, conv_gain, conv_weight, conv_bias, time_weight, time_bias, up_weight,
    up_bias,
):
    vmem = pl.BlockSpec(memory_space=pltpu.VMEM)
    anywhere = pl.BlockSpec(memory_space=pl.ANY)
    return pl.pallas_call(
        kernel,
        out_shape=jax.ShapeDtypeStruct((2, 4, 2 * COLS, C // 2), BF16),
        in_specs=[
            anywhere, vmem, anywhere, anywhere, vmem, anywhere, vmem, anywhere, vmem, anywhere, vmem,
        ],
        out_specs=vmem,
        scratch_shapes=[
            pltpu.VMEM((PARTS, PART, C), BF16),
            pltpu.VMEM((4 * PARTS, 4, PART, C), BF16),
            pltpu.VMEM((2 * OWN, C), BF16),
            pltpu.VMEM((2 * OWN, C), F32),
            pltpu.VMEM((2 * OWN, 128), F32),
            pltpu.VMEM((2 * OWN, 128), F32),
            pltpu.VMEM((OWN, C), F32),
            pltpu.VMEM((OWN, 128), F32),
            pltpu.VMEM((OWN, 128), F32),
            pltpu.VMEM((C, 3 * C), BF16),
            pltpu.VMEM((C, C), BF16),
            pltpu.VMEM((3, 3, C, 3 * C), BF16),
            pltpu.VMEM((3, C, 2 * C), BF16),
            pltpu.VMEM((3, 3, C // 2, C), BF16),
            pltpu.VMEM((2, 2 * C, 2 * C), BF16),
            pltpu.VMEM((2, COLS, C), BF16),
            pltpu.VMEM((2, COLS, C), BF16),
            pltpu.VMEM((3, 4, COLS, C), BF16),
            pltpu.VMEM((2 * COLS, 3 * C), F32),
            pltpu.VMEM((3, 2 * COLS, C), BF16),
            pltpu.VMEM((4, 2, COLS, C), BF16),
            pltpu.VMEM((2, 2 * COLS, 128), F32),
            pltpu.SemaphoreType.DMA((SENDS,)),
            pltpu.SemaphoreType.DMA((SENDS,)),
            pltpu.SemaphoreType.DMA((LOADS,)),
        ],
        compiler_params=pltpu.CompilerParams(
            collective_id=0, has_side_effects=True, vmem_limit_bytes=56 * 1024 * 1024
        ),
    )(
        latent, attn_gain, qkv_weight, proj_weight, conv_gain, conv_weight, conv_bias, time_weight, time_bias,
        jnp.swapaxes(up_weight, 2, 3), up_bias,
    )


def solution(mesh):
    return jax.shard_map(
        body,
        mesh=mesh,
        in_specs=(P("tm", "space", None, None), P(), P(), P(), P(), P(), P(), P(), P(), P(), P()),
        out_specs=P("tm", "space", None, None),
        check_vma=False,
    )
```

time: 115 us -> 82 us (0.71)
  Pallas kernels: 95.3 us -> 78.1 us
  other arithmetic: 10.5 us -> 0 us
  local copies, waits for them, and re-layouts: 8.1 us -> 2.47 us
    pallas_call x1, Pallas kernels: 95.3 us -> 78.1 us  [body(): pl.pallas_call(kernel, out_shape=jax.ShapeDtypeStruct((2, 4, 2 * COLS, C...]
    another operation x2 -> x0, other arithmetic: 9.42 us -> none  [up_table(): jnp.stack([jnp.concatenate([jnp.concatenate([cell(a, b, e, f) for b, f in...]
    broadcast_in_dim x5 -> x0, local copies, waits for them, and re-layouts: 2.91 us -> none  [the longest x1 0.6 us: body(): conv_gain[None]]
    unnamed x11 -> x0, local copies, waits for them, and re-layouts: 2.55 us -> none
where the time goes in v1:
time: 82 us; the launch traced here: 80.6 us
  Pallas kernels  78.1 us (95%)
  local copies, waits for them, and re-layouts  2.47 us (3%)
    pallas_call x1, Pallas kernels, body(): pl.pallas_call(kernel, out_shape=jax.ShapeDtypeStruct((2, 4, 2 * COLS, C...  78.1 us
    pallas_call x1, local copies, waits for them, and re-layouts, body(): pl.pallas_call(kernel, out_shape=jax.ShapeDtypeStruct((2, 4, 2 * COLS, C...  2.47 us

profile of v1, /device:TPU:1, one launch (start us, length us, event | category | flops | bytes accessed | tf_op | source)
XLA Modules:
  0.0 80.6 jit_solution(725155364555935848)
XLA Ops:
  0.0 78.1 %shard_map.109 = bf16[2,4,320,192]{3,2,1,0:T(8,128)(2,1)} custom-call(bf16[1,2,160,384]{3,2,1,0:T(8,128)(2,1)} %latent.1, f32[384]{0:T(512)} %attn_gain.1, bf16[384,1152]{1,0:T(8,128)(2,1)} %qkv_hbm.1, bf16[384,384]{1,0:T(8,128)(2,1)} %proj_hbm.1, f32[384]{0:T(512)} %conv_gain.1, bf16[3,3,3,384,384]{4,3,2,1,0:T(8,128)(2,1)} %conv_hbm.1, f32[384]{0:T(512)} %conv_bias.1, ...), custom_call_target="tpu_custom_call" | custom-call | tf_op jit(solution)/shard_map/pallas_call | solution.py:353
  78.1 2.5 %copy.12 = bf16[2,4,320,192]{2,3,1,0:T(8,128)(2,1)} copy(bf16[2,4,320,192]{3,2,1,0:T(8,128)(2,1)} %shard_map.109) | data formatting | bytes 1966080 | tf_op jit(solution)/shard_map/pallas_call | solution.py:353

commit v2 on v1

--- a/solution.py
+++ b/solution.py
@@ -17,6 +17,7 @@
 PART = 80
 OWN = PARTS * PART
 SIDES = (0, 3, 1, 2)
+TIMES = (0, 2, 1)
 ORDER = (
     ("own", 0), ("own", 1), ("f+", 0), ("f-", 0), ("g+", 0, 0), ("g-", 0, 0), ("own", 2), ("f-", 1), ("g-", 1, 0),
     ("g-", 0, 3), ("g-", 0, 1), ("f+", 1), ("g+", 1, 0), ("own", 3), ("f-", 2), ("g-", 2, 0), ("g+", 0, 3),
@@ -89,8 +90,6 @@
     z_minus = at(lax.rem(z + 7, 8), s)
     z_plus2 = at(lax.rem(z + 2, 8), s)
     z_minus2 = at(lax.rem(z + 6, 8), s)
-    s_up = at(z, lax.rem(s + 31, 32))
-    s_down = at(z, lax.rem(s + 1, 32))
 
     pending = []
     local = []
@@ -123,9 +122,10 @@
     ]
     proj_load = load(proj_hbm, proj)
     conv_loads = [
-        [load(conv_hbm.at[dt, :, dx], wc.at[dt, :, :, pl.ds(dx * C, C)]) for dx in range(3)] for dt in range(3)
+        [load(conv_hbm.at[dt, :, dx], wc.at[TIMES.index(dt), :, :, pl.ds(dx * C, C)]) for dx in range(3)]
+        for dt in TIMES
     ]
-    time_load = load(time_hbm, wt)
+    time_loads = [load(time_hbm.at[dt], wt.at[TIMES.index(dt)]) for dt in TIMES]
     up_load = load(up_hbm, up)
 
     mx[...] = jnp.full(mx.shape, -1e30, F32)
@@ -240,102 +240,131 @@
     act[1, 1:3] = silu(rms(value, conv_gain[...].reshape(1, C))).astype(BF16).reshape(2, COLS, C)
 
 
-    to_next = send(act.at[1, 1:3], act.at[0, 1:3], z_plus)
-    to_previous = send(mid, mid_in, z_minus)
-
-    def edges(f):
-        return [send(act.at[f, 1], act.at[f, 3], s_up), send(act.at[f, 2], act.at[f, 0], s_down)]
-
-    def settle(copies, f):
-        for copy in copies:
+    far_own, near_own = 1 + core, 2 - core
+    far_halo, near_halo = 3 * core, 3 - 3 * core
+    edge = lax.rem(s, 31) == 0
+
+    def to_far(buffer):
+        return send(buffer.at[far_own], buffer.at[near_halo], far)
+
+    def to_near(buffer):
+        return send(buffer.at[near_own], buffer.at[far_halo], sib)
+
+    def beside(own):
+        return (
+            send(act.at[1, own], act.at[0, own], z_plus),
+            send(mid.at[own - 1], mid_in.at[own - 1], z_minus),
+        )
+
+    def arrived(pair, own, forward):
+        pair[0].wait_recv()
+        older = forward(act.at[0])
+        pair[1].wait_recv()
+        act[2, own] = silu(rms(mid_in[own - 1], conv_gain[...].reshape(1, C))).astype(BF16)
+        return older, forward(act.at[2])
+
+    def close(f):
+        @pl.when(edge)
+        def _():
+            act[f, far_halo] = jnp.zeros((COLS, C), BF16)
+
+    def taps(f, own):
+        return jnp.concatenate([act[f, own - 1 + dy] for dy in range(3)], axis=1)
+
+    def convolve(own):
+        older = taps(0, own)
+        older = jnp.where((z != 1) & (z != 2), older, jnp.zeros_like(older))
+        both = jnp.concatenate([older, taps(2, own)], axis=1)
+        value = conv[own - 1] + dot(both, wc[0:2].reshape(6 * C, 3 * C))
+        value = value[:, C : 2 * C] + moved(value[:, :C], 1) + moved(value[:, 2 * C :], -1)
+        value = value + conv_bias[...].reshape(1, C) + mid_in[own - 1].astype(F32)
+        blocks[1, own - 1] = value.astype(BF16)
+
+    def spread(own):
+        return (
+            send(blocks.at[1, own - 1], blocks.at[0, own - 1], z_plus),
+            send(blocks.at[1, own - 1], blocks.at[2, own - 1], z_minus),
+        )
+
+    def double(pair, own):
+        for copy in pair:
             copy.wait_recv()
-
-        @pl.when(s == 0)
-        def _():
-            act[f, 0] = jnp.zeros((COLS, C), BF16)
-
-        @pl.when(s == 31)
-        def _():
-            act[f, 3] = jnp.zeros((COLS, C), BF16)
-
-    def convolve(f):
-        taps = jnp.concatenate([flat(act[f, dy : dy + 2]) for dy in range(3)], axis=1)
-        conv[...] += dot(taps, wc[f].reshape(3 * C, 3 * C))
-
-    halo = {1: edges(1)}
-    conv[...] = jnp.zeros(conv.shape, F32)
-    for row in conv_loads:
-        for copy in row:
-            copy.wait()
-    settle(halo[1], 1)
-
-    @pl.when(z != 1)
-    def _():
-        convolve(1)
-
-    to_next.wait_recv()
-    halo[0] = edges(0)
-    to_previous.wait_recv()
-    act[2, 1:3] = silu(rms(flat(mid_in[...]), conv_gain[...].reshape(1, C))).astype(BF16).reshape(2, COLS, C)
-    halo[2] = edges(2)
-    settle(halo[0], 0)
-
-    @pl.when((z != 1) & (z != 2))
-    def _():
-        convolve(0)
-
-    settle(halo[2], 2)
-    convolve(2)
-    value = conv[:, C : 2 * C] + moved(conv[:, :C], 1) + moved(conv[:, 2 * C :], -1)
-    value = (value + conv_bias[...].reshape(1, C) + flat(mid_in[...]).astype(F32)).astype(BF16)
-    blocks[1] = value
-    next_block = send(blocks.at[1], blocks.at[0], z_plus)
-    previous_block = send(blocks.at[1], blocks.at[2], z_minus)
-    time_load.wait()
-    total = dot(jnp.where(z >= 1, value, jnp.zeros_like(value)), wt[1]) + time_bias[...].reshape(1, 2 * C)
-    next_block.wait_recv()
-    total += dot(jnp.where(z >= 2, blocks[0], jnp.zeros_like(value)), wt[0])
-    previous_block.wait_recv()
-    total += dot(blocks[2], wt[2])
-    doubled = total.astype(BF16).reshape(2, COLS, 2 * C)
-    frames[1:3, 0] = doubled[:, :, :C]
-    frames[1:3, 1] = doubled[:, :, C:]
-    above = send(frames.at[1], frames.at[3], s_up)
-    below = send(frames.at[2], frames.at[0], s_down)
+        older = blocks[0, own - 1]
+        older = jnp.where(z >= 2, older, jnp.zeros_like(older))
+        both = jnp.concatenate([older, blocks[2, own - 1]], axis=1)
+        value = (conv[own - 1, :, : 2 * C] + dot(both, wt[0:2].reshape(2 * C, 2 * C))).astype(BF16)
+        frames[own, 0] = value[:, :C]
+        frames[own, 1] = value[:, C:]
 
     bias = up_bias[...].reshape(1, C // 2)
 
     def upsample(i, a):
-        taps = jnp.concatenate([flat(frames[i + a]), flat(frames[i + a + 1])], axis=1)
-        value = lax.dot_general(taps, wu[a], NT, preferred_element_type=F32)
+        rows = jnp.concatenate([flat(frames[i + a]), flat(frames[i + a + 1])], axis=1)
+        value = lax.dot_general(rows, wu[a], NT, preferred_element_type=F32)
         side = value[:, C:]
         lane = lax.broadcasted_iota(jnp.int32, side.shape, 1)
         value = value[:, :C] + jnp.where(lane < C // 2, moved(side, 1), moved(side, -1))
         second = pltpu.roll(value, C // 2, 1)
         for frame in range(2):
-            rows = slice(frame * COLS, (frame + 1) * COLS)
+            run = slice(frame * COLS, (frame + 1) * COLS)
             for part in range(2):
                 lanes = slice(128 * part, 128 * part + 128)
-                wide[part, pl.ds(0, COLS, stride=2), :] = value[rows, lanes]
-                wide[part, pl.ds(1, COLS, stride=2), :] = second[rows, lanes]
+                wide[part, pl.ds(0, COLS, stride=2), :] = value[run, lanes]
+                wide[part, pl.ds(1, COLS, stride=2), :] = second[run, lanes]
             out[frame, 2 * i + a, :, :128] = (wide[0] + bias[:, :128]).astype(BF16)
             out[frame, 2 * i + a, :, 128:] = (wide[1, :, : C // 2 - 128] + bias[:, 128:]).astype(BF16)
 
+    far_pair = beside(far_own)
+    own_edges = to_far(act.at[1]), to_near(act.at[1])
+    near_pair = beside(near_own)
+    for row in conv_loads:
+        for copy in row:
+            copy.wait()
+    for copy in own_edges:
+        copy.wait_recv()
+    close(1)
+
+    @pl.when(z != 1)
+    def _():
+        rows = jnp.concatenate([flat(act[1, dy : dy + 2]) for dy in range(3)], axis=1)
+        conv[...] = dot(rows, wc[2].reshape(3 * C, 3 * C)).reshape(conv.shape)
+
+    @pl.when(z == 1)
+    def _():
+        conv[...] = jnp.zeros(conv.shape, F32)
+
+    far_edges = arrived(far_pair, far_own, to_far)
+    near_edges = arrived(near_pair, near_own, to_near)
+    for copy in near_edges:
+        copy.wait_recv()
+    convolve(near_own)
+    for copy in far_edges:
+        copy.wait_recv()
+    close(0)
+    close(2)
+    convolve(far_own)
+    far_pair = spread(far_own)
+    near_pair = spread(near_own)
+    for copy in time_loads:
+        copy.wait()
+    rows = flat(blocks[1])
+    rows = jnp.where(z >= 1, rows, jnp.zeros_like(rows))
+    conv[:, :, : 2 * C] = (dot(rows, wt[2]) + time_bias[...].reshape(1, 2 * C)).reshape(2, COLS, 2 * C)
+    double(far_pair, far_own)
+    far_edge = to_far(frames)
+    double(near_pair, near_own)
+    near_edge = to_near(frames)
     upsample(0, 1)
     upsample(1, 0)
-    above.wait_recv()
-    below.wait_recv()
-
-    @pl.when(s == 0)
+    near_edge.wait_recv()
+    upsample(1 - core, 1 - core)
+    far_edge.wait_recv()
+
+    @pl.when(edge)
     def _():
-        frames[0] = jnp.zeros((2, COLS, C), BF16)
-
-    @pl.when(s == 31)
-    def _():
-        frames[3] = jnp.zeros((2, COLS, C), BF16)
-
-    upsample(0, 0)
-    upsample(1, 1)
+        frames[far_halo] = jnp.zeros((2, COLS, C), BF16)
+
+    upsample(core, core)
     for copy in pending:
         copy.wait_send()
 
@@ -376,8 +405,8 @@
             pltpu.VMEM((2, COLS, C), BF16),
             pltpu.VMEM((2, COLS, C), BF16),
             pltpu.VMEM((3, 4, COLS, C), BF16),
-            pltpu.VMEM((2 * COLS, 3 * C), F32),
-            pltpu.VMEM((3, 2 * COLS, C), BF16),
+            pltpu.VMEM((2, COLS, 3 * C), F32),
+            pltpu.VMEM((3, 2, COLS, C), BF16),
             pltpu.VMEM((4, 2, COLS, C), BF16),
             pltpu.VMEM((2, 2 * COLS, 128), F32),
             pltpu.SemaphoreType.DMA((SENDS,)),

time: 82 us -> 78.9 us (0.962)
  Pallas kernels: 78.1 us -> 75.3 us
    pallas_call x1, Pallas kernels: 78.1 us -> 75.3 us  [body(): pl.pallas_call(kernel, out_shape=jax.ShapeDtypeStruct((2, 4, 2 * COLS, C...]
where the time goes in v2:
time: 78.9 us; the launch traced here: 77.8 us
  Pallas kernels  75.3 us (95%)
  local copies, waits for them, and re-layouts  2.47 us (3%)
    pallas_call x1, Pallas kernels, body(): pl.pallas_call(kernel, out_shape=jax.ShapeDtypeStruct((2, 4, 2 * COLS, C...  75.3 us
    pallas_call x1, local copies, waits for them, and re-layouts, body(): pl.pallas_call(kernel, out_shape=jax.ShapeDtypeStruct((2, 4, 2 * COLS, C...  2.47 us

profile of v2, /device:TPU:1, one launch (start us, length us, event | category | flops | bytes accessed | tf_op | source)
XLA Modules:
  0.0 77.8 jit_solution(5784031687948620400)
XLA Ops:
  0.0 75.3 %shard_map.109 = bf16[2,4,320,192]{3,2,1,0:T(8,128)(2,1)} custom-call(bf16[1,2,160,384]{3,2,1,0:T(8,128)(2,1)} %latent.1, f32[384]{0:T(512)} %attn_gain.1, bf16[384,1152]{1,0:T(8,128)(2,1)} %qkv_hbm.1, bf16[384,384]{1,0:T(8,128)(2,1)} %proj_hbm.1, f32[384]{0:T(512)} %conv_gain.1, bf16[3,3,3,384,384]{4,3,2,1,0:T(8,128)(2,1)} %conv_hbm.1, f32[384]{0:T(512)} %conv_bias.1, ...), custom_call_target="tpu_custom_call" | custom-call | tf_op jit(solution)/shard_map/pallas_call | solution.py:382
  75.3 2.5 %copy.12 = bf16[2,4,320,192]{2,3,1,0:T(8,128)(2,1)} copy(bf16[2,4,320,192]{3,2,1,0:T(8,128)(2,1)} %shard_map.109) | data formatting | bytes 1966080 | tf_op jit(solution)/shard_map/pallas_call | solution.py:382

commit v3 on v2

--- a/solution.py
+++ b/solution.py
@@ -16,19 +16,20 @@
 PARTS = 4
 PART = 80
 OWN = PARTS * PART
+HALF = 80
 SIDES = (0, 3, 1, 2)
 TIMES = (0, 2, 1)
 ORDER = (
-    ("own", 0), ("own", 1), ("f+", 0), ("f-", 0), ("g+", 0, 0), ("g-", 0, 0), ("own", 2), ("f-", 1), ("g-", 1, 0),
-    ("g-", 0, 3), ("g-", 0, 1), ("f+", 1), ("g+", 1, 0), ("own", 3), ("f-", 2), ("g-", 2, 0), ("g+", 0, 3),
-    ("op", 0), ("g+", 0, 1), ("go", 0, 0), ("query", 0), ("f+", 2), ("g+", 2, 0), ("attend", 0, 0, 1), ("g+", 1, 1),
-    ("g-", 1, 1), ("op", 1), ("g+", 1, 3), ("go", 1, 0), ("go", 0, 3), ("go", 0, 1), ("f+", 3), ("g+", 3, 0),
-    ("g+", 2, 1), ("g+", 0, 2), ("g-", 1, 3), ("f-", 3), ("g-", 3, 0), ("g-", 2, 1), ("g-", 0, 2),
-    ("attend", 0, 1, 2), ("table", 0), ("g-", 2, 3), ("g-", 1, 2), ("g+", 2, 3), ("op", 2), ("go", 2, 0),
-    ("g-", 3, 3), ("go", 1, 1), ("g+", 1, 2), ("attend", 1, 1, 2), ("go", 1, 3), ("g+", 3, 3), ("go", 0, 2),
-    ("g+", 3, 1), ("g+", 2, 2), ("g-", 3, 1), ("op", 3), ("go", 3, 0), ("go", 2, 1), ("attend", 0, 3, 2),
-    ("go", 2, 3), ("go", 1, 2), ("g-", 2, 2), ("attend", 1, 3, 2), ("g-", 3, 2), ("attend", 2, 1, 2), ("go", 3, 3),
-    ("go", 3, 1), ("go", 2, 2), ("g+", 3, 2), ("attend", 2, 3, 2), ("go", 3, 2), ("attend", 3, 1, 2),
+    ("own", 0), ("own", 1), ("f-", 0), ("f+", 0), ("own", 2), ("f-", 1), ("own", 3), ("f+", 1), ("op", 1),
+    ("g+", 0, 1), ("g+", 1, 0), ("op", 0), ("query", 0), ("g-", 0, 3), ("f+", 2), ("attend", 0, 0, 1), ("g+", 0, 3),
+    ("g-", 0, 0), ("g-", 2, 0), ("g+", 0, 0), ("g-", 1, 3), ("g+", 3, 0), ("g-", 1, 0), ("g+", 1, 1), ("g+", 1, 3),
+    ("g-", 1, 1), ("g-", 1, 2), ("g+", 1, 2), ("f-", 3), ("attend", 1, 1, 2), ("table", 0), ("g-", 0, 2),
+    ("go", 0, 3), ("g+", 0, 2), ("g-", 0, 1), ("op", 2), ("attend", 0, 1, 2), ("f+", 3), ("g+", 2, 3), ("go", 0, 0),
+    ("f-", 2), ("go", 1, 0), ("g-", 2, 3), ("g+", 2, 0), ("go", 1, 1), ("go", 1, 3), ("go", 1, 2),
+    ("attend", 1, 3, 2), ("op", 3), ("g+", 3, 1), ("go", 0, 2), ("g-", 3, 0), ("go", 0, 1), ("attend", 0, 3, 2),
+    ("g+", 3, 3), ("g-", 3, 3), ("g-", 2, 2), ("g+", 2, 2), ("g-", 3, 1), ("g-", 2, 1), ("g+", 2, 1),
+    ("attend", 2, 1, 2), ("go", 2, 3), ("g-", 3, 2), ("g+", 3, 2), ("go", 2, 0), ("go", 3, 0), ("attend", 3, 1, 2),
+    ("go", 3, 3), ("go", 2, 1), ("go", 2, 2), ("attend", 2, 3, 2), ("go", 3, 2), ("go", 3, 1),
 )
 
 
@@ -60,9 +61,10 @@
 
 
 def kernel(
-    latent, attn_gain, qkv_hbm, proj_hbm, conv_gain, conv_hbm, conv_bias, time_hbm, time_bias, up_hbm, up_bias,
-    out,
-    lat, nb, qb, acc, mx, den, acc_in, mx_in, den_in,
+    latent, attn_gain_hbm, qkv_hbm, proj_hbm, conv_gain_hbm, conv_hbm, conv_bias_hbm, time_hbm, time_bias_hbm, up_hbm,
+    up_bias_hbm, out_hbm,
+    attn_gain, conv_gain, conv_bias, time_bias, up_bias, out,
+    lat, nb, qb, acc, mx, den, acc_out, stat_out, acc_in, stat_in,
     qkv, proj, wc, wt, up, wu,
     mid, mid_in, act, conv, blocks, frames, wide,
     ss, rs, ws,
@@ -114,6 +116,7 @@
     partners = (sib, far, f_plus, f_minus, g_plus, g_minus, z_plus, z_minus, z_plus2, z_minus2)
     for partner in partners:
         pl.semaphore_signal(barrier, inc=1, device_id=partner, device_id_type=MESH)
+    gain_load = load(attn_gain_hbm, attn_gain)
     qkv_load = load(qkv_hbm, qkv)
     pl.semaphore_wait(barrier, len(partners))
 
@@ -127,6 +130,12 @@
     ]
     time_loads = [load(time_hbm.at[dt], wt.at[TIMES.index(dt)]) for dt in TIMES]
     up_load = load(up_hbm, up)
+    small_loads = [
+        load(conv_gain_hbm, conv_gain),
+        load(conv_bias_hbm, conv_bias),
+        load(time_bias_hbm, time_bias),
+        load(up_bias_hbm, up_bias),
+    ]
 
     mx[...] = jnp.full(mx.shape, -1e30, F32)
     den[...] = jnp.zeros(den.shape, F32)
@@ -205,35 +214,34 @@
                     cell = summed([rows[dx] for dx in spans[b, f]]).astype(BF16)
                     wu[a, k * C // 2 : (k + 1) * C // 2, e * C : (e + 1) * C] = cell
 
+    gain_load.wait()
     for kind, c, *rest in ORDER:
         if kind == "query":
             q_copy = project()
         elif kind == "attend":
+            if q_copy is not None:
+                q_copy = q_copy.wait_recv()
             attend(c, *rest)
         elif kind == "table":
             up_load.wait()
             table()
         else:
             step(kind, c, *rest)
-            if (kind, c) == ("g+", 2) and rest == [0]:
-                q_copy.wait_recv()
     attend(PARTS - 1, 3, 1, OWN, OWN)
-    back = [
-        send(acc.at[pl.ds(OWN, OWN)], acc_in, sib),
-        send(mx.at[pl.ds(OWN, OWN)], mx_in, sib),
-        send(den.at[pl.ds(OWN, OWN)], den_in, sib),
-    ]
+    acc_out[...] = acc[OWN:].astype(BF16)
+    lane = lax.broadcasted_iota(jnp.int32, (OWN, 128), 1)
+    stat_out[...] = jnp.where(lane < 64, mx[OWN:], jnp.sum(den[OWN:], axis=1, keepdims=True))
+    back = [send(acc_out, acc_in, sib), send(stat_out, stat_in, sib)]
     attend(PARTS - 1, 3, 1, 0, OWN)
-    proj_load.wait()
+    for copy in [proj_load] + small_loads:
+        copy.wait()
     for copy in back:
         copy.wait_recv()
-    top = jnp.maximum(mx[:OWN], mx_in[...])
-    mine = jnp.exp2(mx[:OWN] - top)
-    other = jnp.exp2(mx_in[...] - top)
-    total = jnp.sum(den[:OWN] * mine + den_in[...] * other, axis=1, keepdims=True)
-    mine = jnp.tile(mine / total, (1, C // 128))
-    other = jnp.tile(other / total, (1, C // 128))
-    pooled = (acc[:OWN] * mine + acc_in[...] * other).astype(BF16)
+    top = jnp.maximum(mx[:OWN, :1], stat_in[:, :1])
+    mine = jnp.exp2(mx[:OWN, :1] - top)
+    other = jnp.exp2(stat_in[:, :1] - top)
+    total = jnp.sum(den[:OWN], axis=1, keepdims=True) * mine + stat_in[:, 64:65] * other
+    pooled = (acc[:OWN] * (mine / total) + acc_in[...].astype(F32) * (other / total)).astype(BF16)
     attn = dot(pooled, qkv[:, 2 * C :]).astype(BF16)
     value = (flat(lat[...]).astype(F32) + dot(attn, proj[...])).astype(BF16)
     mid[...] = value.reshape(2, COLS, C)
@@ -250,18 +258,21 @@
     def to_near(buffer):
         return send(buffer.at[near_own], buffer.at[far_halo], sib)
 
-    def beside(own):
+    def halves():
+        return [pl.ds(0, HALF), pl.ds(HALF, HALF)]
+
+    def beside(own, run):
         return (
-            send(act.at[1, own], act.at[0, own], z_plus),
-            send(mid.at[own - 1], mid_in.at[own - 1], z_minus),
+            send(act.at[1, own, run], act.at[0, own, run], z_plus),
+            send(mid.at[own - 1, run], mid_in.at[own - 1, run], z_minus),
         )
 
-    def arrived(pair, own, forward):
+    def arrived(pair, own, run, halo, device):
         pair[0].wait_recv()
-        older = forward(act.at[0])
+        older = send(act.at[0, own, run], act.at[0, halo, run], device)
         pair[1].wait_recv()
-        act[2, own] = silu(rms(mid_in[own - 1], conv_gain[...].reshape(1, C))).astype(BF16)
-        return older, forward(act.at[2])
+        act[2, own, run] = silu(rms(mid_in[own - 1, run], conv_gain[...].reshape(1, C))).astype(BF16)
+        return older, send(act.at[2, own, run], act.at[2, halo, run], device)
 
     def close(f):
         @pl.when(edge)
@@ -280,23 +291,26 @@
         value = value + conv_bias[...].reshape(1, C) + mid_in[own - 1].astype(F32)
         blocks[1, own - 1] = value.astype(BF16)
 
-    def spread(own):
+    def spread(own, run):
         return (
-            send(blocks.at[1, own - 1], blocks.at[0, own - 1], z_plus),
-            send(blocks.at[1, own - 1], blocks.at[2, own - 1], z_minus),
+            send(blocks.at[1, own - 1, run], blocks.at[0, own - 1, run], z_plus),
+            send(blocks.at[1, own - 1, run], blocks.at[2, own - 1, run], z_minus),
         )
 
-    def double(pair, own):
+    def double(pair, own, run, halo, device):
         for copy in pair:
             copy.wait_recv()
-        older = blocks[0, own - 1]
+        older = blocks[0, own - 1, run]
         older = jnp.where(z >= 2, older, jnp.zeros_like(older))
-        both = jnp.concatenate([older, blocks[2, own - 1]], axis=1)
-        value = (conv[own - 1, :, : 2 * C] + dot(both, wt[0:2].reshape(2 * C, 2 * C))).astype(BF16)
-        frames[own, 0] = value[:, :C]
-        frames[own, 1] = value[:, C:]
+        both = jnp.concatenate([older, blocks[2, own - 1, run]], axis=1)
+        value = (conv[own - 1, run, : 2 * C] + dot(both, wt[0:2].reshape(2 * C, 2 * C))).astype(BF16)
+        frames[own, 0, run] = value[:, :C]
+        frames[own, 1, run] = value[:, C:]
+        return send(frames.at[own, :, run], frames.at[halo, :, run], device)
 
     bias = up_bias[...].reshape(1, C // 2)
+
+    stores = []
 
     def upsample(i, a):
         rows = jnp.concatenate([flat(frames[i + a]), flat(frames[i + a + 1])], axis=1)
@@ -313,10 +327,12 @@
                 wide[part, pl.ds(1, COLS, stride=2), :] = second[run, lanes]
             out[frame, 2 * i + a, :, :128] = (wide[0] + bias[:, :128]).astype(BF16)
             out[frame, 2 * i + a, :, 128:] = (wide[1, :, : C // 2 - 128] + bias[:, 128:]).astype(BF16)
-
-    far_pair = beside(far_own)
+        stores.append(load(out.at[:, 2 * i + a], out_hbm.at[:, 2 * i + a]))
+
+    whole = pl.ds(0, COLS)
+    far_pairs = [beside(far_own, run) for run in halves()]
     own_edges = to_far(act.at[1]), to_near(act.at[1])
-    near_pair = beside(near_own)
+    near_pair = beside(near_own, whole)
     for row in conv_loads:
         for copy in row:
             copy.wait()
@@ -333,8 +349,10 @@
     def _():
         conv[...] = jnp.zeros(conv.shape, F32)
 
-    far_edges = arrived(far_pair, far_own, to_far)
-    near_edges = arrived(near_pair, near_own, to_near)
+    far_edges = []
+    for pair, run in zip(far_pairs, halves()):
+        far_edges += arrived(pair, far_own, run, near_halo, far)
+    near_edges = arrived(near_pair, near_own, whole, far_halo, sib)
     for copy in near_edges:
         copy.wait_recv()
     convolve(near_own)
@@ -343,22 +361,21 @@
     close(0)
     close(2)
     convolve(far_own)
-    far_pair = spread(far_own)
-    near_pair = spread(near_own)
+    far_pairs = [spread(far_own, run) for run in halves()]
+    near_pair = spread(near_own, whole)
     for copy in time_loads:
         copy.wait()
     rows = flat(blocks[1])
     rows = jnp.where(z >= 1, rows, jnp.zeros_like(rows))
     conv[:, :, : 2 * C] = (dot(rows, wt[2]) + time_bias[...].reshape(1, 2 * C)).reshape(2, COLS, 2 * C)
-    double(far_pair, far_own)
-    far_edge = to_far(frames)
-    double(near_pair, near_own)
-    near_edge = to_near(frames)
+    far_edges = [double(pair, far_own, run, near_halo, far) for pair, run in zip(far_pairs, halves())]
+    near_edge = double(near_pair, near_own, whole, far_halo, sib)
     upsample(0, 1)
     upsample(1, 0)
     near_edge.wait_recv()
     upsample(1 - core, 1 - core)
-    far_edge.wait_recv()
+    for copy in far_edges:
+        copy.wait_recv()
 
     @pl.when(edge)
     def _():
@@ -367,34 +384,40 @@
     upsample(core, core)
     for copy in pending:
         copy.wait_send()
+    for copy in stores:
+        copy.wait()
 
 
 SENDS = 96
-LOADS = 16
+LOADS = 32
 
 
 def body(
     latent, attn_gain, qkv_weight, proj_weight, conv_gain, conv_weight, conv_bias, time_weight, time_bias, up_weight,
     up_bias,
 ):
-    vmem = pl.BlockSpec(memory_space=pltpu.VMEM)
     anywhere = pl.BlockSpec(memory_space=pl.ANY)
     return pl.pallas_call(
         kernel,
         out_shape=jax.ShapeDtypeStruct((2, 4, 2 * COLS, C // 2), BF16),
-        in_specs=[
-            anywhere, vmem, anywhere, anywhere, vmem, anywhere, vmem, anywhere, vmem, anywhere, vmem,
-        ],
-        out_specs=vmem,
+        in_specs=[anywhere] * 11,
+        out_specs=anywhere,
         scratch_shapes=[
+            pltpu.VMEM((C,), F32),
+            pltpu.VMEM((C,), F32),
+            pltpu.VMEM((C,), F32),
+            pltpu.VMEM((2 * C,), F32),
+            pltpu.VMEM((C // 2,), F32),
+            pltpu.VMEM((2, 4, 2 * COLS, C // 2), BF16),
             pltpu.VMEM((PARTS, PART, C), BF16),
             pltpu.VMEM((4 * PARTS, 4, PART, C), BF16),
             pltpu.VMEM((2 * OWN, C), BF16),
             pltpu.VMEM((2 * OWN, C), F32),
             pltpu.VMEM((2 * OWN, 128), F32),
             pltpu.VMEM((2 * OWN, 128), F32),
-            pltpu.VMEM((OWN, C), F32),
+            pltpu.VMEM((OWN, C), BF16),
             pltpu.VMEM((OWN, 128), F32),
+            pltpu.VMEM((OWN, C), BF16),
             pltpu.VMEM((OWN, 128), F32),
             pltpu.VMEM((C, 3 * C), BF16),
             pltpu.VMEM((C, C), BF16),

time: 78.9 us -> 75.9 us (0.962); the launches traced: 77.8 us -> 75.8 us
  Pallas kernels: 75.3 us -> 73.3 us
    pallas_call x1, Pallas kernels: 75.3 us -> 73.3 us  [body(): pl.pallas_call(kernel, out_shape=jax.ShapeDtypeStruct((2, 4, 2 * COLS, C...]
where the time goes in v3:
time: 75.9 us; the launch traced here: 75.8 us
  Pallas kernels  73.3 us (97%)
  local copies, waits for them, and re-layouts  2.47 us (3%)
    pallas_call x1, Pallas kernels, body(): pl.pallas_call(kernel, out_shape=jax.ShapeDtypeStruct((2, 4, 2 * COLS, C...  73.3 us
    pallas_call x1, local copies, waits for them, and re-layouts, body(): pl.pallas_call(kernel, out_shape=jax.ShapeDtypeStruct((2, 4, 2 * COLS, C...  2.47 us

profile of v3, /device:TPU:1, one launch (start us, length us, event | category | flops | bytes accessed | tf_op | source)
XLA Modules:
  0.0 75.8 jit_solution(12015019157664697764)
XLA Ops:
  0.0 73.3 %shard_map.109 = bf16[2,4,320,192]{3,2,1,0:T(8,128)(2,1)} custom-call(bf16[1,2,160,384]{3,2,1,0:T(8,128)(2,1)} %latent.1, f32[384]{0:T(512)} %attn_gain_hbm.1, bf16[384,1152]{1,0:T(8,128)(2,1)} %qkv_hbm.1, bf16[384,384]{1,0:T(8,128)(2,1)} %proj_hbm.1, f32[384]{0:T(512)} %conv_gain_hbm.1, bf16[3,3,3,384,384]{4,3,2,1,0:T(8,128)(2,1)} %conv_hbm.1, ...), custom_call_target="tpu_custom_call" | custom-call | tf_op jit(solution)/shard_map/pallas_call | solution.py:400
  73.3 2.5 %copy.12 = bf16[2,4,320,192]{2,3,1,0:T(8,128)(2,1)} copy(bf16[2,4,320,192]{3,2,1,0:T(8,128)(2,1)} %shard_map.109) | data formatting | bytes 1966080 | tf_op jit(solution)/shard_map/pallas_call | solution.py:400

commit v4 on v3

--- a/solution.py
+++ b/solution.py
@@ -105,6 +105,13 @@
         pending.append(copy)
         return copy
 
+    left = []
+
+    def sent(*copies):
+        for copy in copies:
+            copy.wait_send()
+            left.append(id(copy))
+
 
     def load(src, dst):
         copy = pltpu.make_async_copy(src, dst, ws.at[len(local)])
@@ -120,9 +127,16 @@
     qkv_load = load(qkv_hbm, qkv)
     pl.semaphore_wait(barrier, len(partners))
 
-    shift = [
-        send(latent.at[0, c // 2, pl.ds(c % 2 * PART, PART)], lat.at[c], z_plus2) for c in range(PARTS)
-    ]
+    shift = []
+
+    def shift_next():
+        c = len(shift)
+        if c < PARTS:
+            if c:
+                sent(shift[-1])
+            shift.append(send(latent.at[0, c // 2, pl.ds(c % 2 * PART, PART)], lat.at[c], z_plus2))
+
+    shift_next()
     proj_load = load(proj_hbm, proj)
     conv_loads = [
         [load(conv_hbm.at[dt, :, dx], wc.at[TIMES.index(dt), :, :, pl.ds(dx * C, C)]) for dx in range(3)]
@@ -157,6 +171,7 @@
             copies["f+", c, 0] = send(slot(c, 0, 0), slot(c, 0, 3), f_plus)
             copies["f-", c, 0] = send(slot(c, 0, 0), slot(c, 0, 1), f_minus)
             along_second(c, 0)
+            shift_next()
             return
         copies[kind, c, i].wait_recv()
         if kind == "f+":
@@ -215,6 +230,8 @@
                     wu[a, k * C // 2 : (k + 1) * C // 2, e * C : (e + 1) * C] = cell
 
     gain_load.wait()
+    for _ in range(SHIFT_AHEAD):
+        shift_next()
     for kind, c, *rest in ORDER:
         if kind == "query":
             q_copy = project()
@@ -356,23 +373,25 @@
     for copy in near_edges:
         copy.wait_recv()
     convolve(near_own)
+    near_pair = spread(near_own, halves()[0])
     for copy in far_edges:
         copy.wait_recv()
     close(0)
     close(2)
     convolve(far_own)
     far_pairs = [spread(far_own, run) for run in halves()]
-    near_pair = spread(near_own, whole)
     for copy in time_loads:
         copy.wait()
     rows = flat(blocks[1])
     rows = jnp.where(z >= 1, rows, jnp.zeros_like(rows))
+    near_pairs = [near_pair, spread(near_own, halves()[1])]
     conv[:, :, : 2 * C] = (dot(rows, wt[2]) + time_bias[...].reshape(1, 2 * C)).reshape(2, COLS, 2 * C)
     far_edges = [double(pair, far_own, run, near_halo, far) for pair, run in zip(far_pairs, halves())]
-    near_edge = double(near_pair, near_own, whole, far_halo, sib)
+    near_edges = [double(pair, near_own, run, far_halo, sib) for pair, run in zip(near_pairs, halves())]
     upsample(0, 1)
     upsample(1, 0)
-    near_edge.wait_recv()
+    for copy in near_edges:
+        copy.wait_recv()
     upsample(1 - core, 1 - core)
     for copy in far_edges:
         copy.wait_recv()
@@ -383,11 +402,13 @@
 
     upsample(core, core)
     for copy in pending:
-        copy.wait_send()
+        if id(copy) not in left:
+            copy.wait_send()
     for copy in stores:
         copy.wait()
 
 
+SHIFT_AHEAD = 2
 SENDS = 96
 LOADS = 32
 

time: 75.9 us -> 75 us (0.988)
  Pallas kernels: 73.3 us -> 72.4 us
    pallas_call x1, Pallas kernels: 73.3 us -> 72.4 us  [body(): pl.pallas_call(kernel, out_shape=jax.ShapeDtypeStruct((2, 4, 2 * COLS, C...]
where the time goes in v4:
time: 75 us; the launch traced here: 74.9 us
  Pallas kernels  72.4 us (97%)
  local copies, waits for them, and re-layouts  2.47 us (3%)
    pallas_call x1, Pallas kernels, body(): pl.pallas_call(kernel, out_shape=jax.ShapeDtypeStruct((2, 4, 2 * COLS, C...  72.4 us
    pallas_call x1, local copies, waits for them, and re-layouts, body(): pl.pallas_call(kernel, out_shape=jax.ShapeDtypeStruct((2, 4, 2 * COLS, C...  2.47 us

profile of v4, /device:TPU:1, one launch (start us, length us, event | category | flops | bytes accessed | tf_op | source)
XLA Modules:
  0.0 74.9 jit_solution(14234822449659165705)
XLA Ops:
  0.0 72.4 %shard_map.109 = bf16[2,4,320,192]{3,2,1,0:T(8,128)(2,1)} custom-call(bf16[1,2,160,384]{3,2,1,0:T(8,128)(2,1)} %latent.1, f32[384]{0:T(512)} %attn_gain_hbm.1, bf16[384,1152]{1,0:T(8,128)(2,1)} %qkv_hbm.1, bf16[384,384]{1,0:T(8,128)(2,1)} %proj_hbm.1, f32[384]{0:T(512)} %conv_gain_hbm.1, bf16[3,3,3,384,384]{4,3,2,1,0:T(8,128)(2,1)} %conv_hbm.1, ...), custom_call_target="tpu_custom_call" | custom-call | tf_op jit(solution)/shard_map/pallas_call | solution.py:421
  72.5 2.5 %copy.12 = bf16[2,4,320,192]{2,3,1,0:T(8,128)(2,1)} copy(bf16[2,4,320,192]{3,2,1,0:T(8,128)(2,1)} %shard_map.109) | data formatting | bytes 1966080 | tf_op jit(solution)/shard_map/pallas_call | solution.py:421

commit v5 on v4

--- a/solution.py
+++ b/solution.py
@@ -20,16 +20,16 @@
 SIDES = (0, 3, 1, 2)
 TIMES = (0, 2, 1)
 ORDER = (
-    ("own", 0), ("own", 1), ("f-", 0), ("f+", 0), ("own", 2), ("f-", 1), ("own", 3), ("f+", 1), ("op", 1),
-    ("g+", 0, 1), ("g+", 1, 0), ("op", 0), ("query", 0), ("g-", 0, 3), ("f+", 2), ("attend", 0, 0, 1), ("g+", 0, 3),
-    ("g-", 0, 0), ("g-", 2, 0), ("g+", 0, 0), ("g-", 1, 3), ("g+", 3, 0), ("g-", 1, 0), ("g+", 1, 1), ("g+", 1, 3),
-    ("g-", 1, 1), ("g-", 1, 2), ("g+", 1, 2), ("f-", 3), ("attend", 1, 1, 2), ("table", 0), ("g-", 0, 2),
-    ("go", 0, 3), ("g+", 0, 2), ("g-", 0, 1), ("op", 2), ("attend", 0, 1, 2), ("f+", 3), ("g+", 2, 3), ("go", 0, 0),
-    ("f-", 2), ("go", 1, 0), ("g-", 2, 3), ("g+", 2, 0), ("go", 1, 1), ("go", 1, 3), ("go", 1, 2),
-    ("attend", 1, 3, 2), ("op", 3), ("g+", 3, 1), ("go", 0, 2), ("g-", 3, 0), ("go", 0, 1), ("attend", 0, 3, 2),
-    ("g+", 3, 3), ("g-", 3, 3), ("g-", 2, 2), ("g+", 2, 2), ("g-", 3, 1), ("g-", 2, 1), ("g+", 2, 1),
-    ("attend", 2, 1, 2), ("go", 2, 3), ("g-", 3, 2), ("g+", 3, 2), ("go", 2, 0), ("go", 3, 0), ("attend", 3, 1, 2),
-    ("go", 3, 3), ("go", 2, 1), ("go", 2, 2), ("attend", 2, 3, 2), ("go", 3, 2), ("go", 3, 1),
+    ("own", 0), ("own", 1), ("f+", 0), ("f-", 0), ("own", 2), ("f-", 1), ("g+", 1, 0), ("own", 3), ("op", 0),
+    ("query", 0), ("f+", 1), ("g+", 0, 1), ("g+", 0, 0), ("g+", 0, 3), ("g-", 1, 1), ("op", 1), ("attend", 0, 0, 1),
+    ("g-", 0, 3), ("g-", 0, 0), ("g-", 0, 1), ("f+", 2), ("g+", 3, 0), ("g-", 1, 0), ("g-", 2, 0), ("g+", 0, 2),
+    ("f-", 3), ("g-", 0, 2), ("attend", 0, 1, 2), ("table", 0), ("g-", 1, 2), ("g-", 1, 3), ("g+", 1, 1),
+    ("go", 0, 0), ("g+", 1, 3), ("f-", 2), ("g+", 1, 2), ("attend", 1, 1, 2), ("go", 0, 3), ("g+", 2, 3), ("op", 2),
+    ("go", 0, 1), ("g-", 3, 0), ("g+", 2, 0), ("f+", 3), ("go", 0, 2), ("attend", 0, 3, 2), ("op", 3), ("go", 1, 0),
+    ("g+", 3, 1), ("g-", 2, 3), ("g-", 3, 1), ("go", 1, 1), ("go", 1, 2), ("go", 1, 3), ("attend", 1, 3, 2),
+    ("g+", 2, 2), ("g+", 2, 1), ("g-", 2, 1), ("g-", 2, 2), ("attend", 2, 1, 2), ("go", 2, 0), ("g+", 3, 3),
+    ("g-", 3, 2), ("g-", 3, 3), ("g+", 3, 2), ("attend", 3, 1, 2), ("go", 3, 1), ("go", 2, 3), ("go", 2, 1),
+    ("go", 2, 2), ("attend", 2, 3, 2), ("go", 3, 3), ("go", 3, 0), ("go", 3, 2),
 )
 
 

time: 75 us -> 72.8 us (0.971)
  Pallas kernels: 72.4 us -> 70 us
    pallas_call x1, Pallas kernels: 72.4 us -> 70 us  [body(): pl.pallas_call(kernel, out_shape=jax.ShapeDtypeStruct((2, 4, 2 * COLS, C...]
where the time goes in v5:
time: 72.8 us; the launch traced here: 72.4 us
  Pallas kernels  70 us (96%)
  local copies, waits for them, and re-layouts  2.47 us (3%)
    pallas_call x1, Pallas kernels, body(): pl.pallas_call(kernel, out_shape=jax.ShapeDtypeStruct((2, 4, 2 * COLS, C...  70 us
    pallas_call x1, local copies, waits for them, and re-layouts, body(): pl.pallas_call(kernel, out_shape=jax.ShapeDtypeStruct((2, 4, 2 * COLS, C...  2.47 us

profile of v5, /device:TPU:1, one launch (start us, length us, event | category | flops | bytes accessed | tf_op | source)
XLA Modules:
  0.0 72.4 jit_solution(8999004434830966318)
XLA Ops:
  0.0 70.0 %shard_map.109 = bf16[2,4,320,192]{3,2,1,0:T(8,128)(2,1)} custom-call(bf16[1,2,160,384]{3,2,1,0:T(8,128)(2,1)} %latent.1, f32[384]{0:T(512)} %attn_gain_hbm.1, bf16[384,1152]{1,0:T(8,128)(2,1)} %qkv_hbm.1, bf16[384,384]{1,0:T(8,128)(2,1)} %proj_hbm.1, f32[384]{0:T(512)} %conv_gain_hbm.1, bf16[3,3,3,384,384]{4,3,2,1,0:T(8,128)(2,1)} %conv_hbm.1, ...), custom_call_target="tpu_custom_call" | custom-call | tf_op jit(solution)/shard_map/pallas_call | solution.py:421
  70.0 2.5 %copy.12 = bf16[2,4,320,192]{2,3,1,0:T(8,128)(2,1)} copy(bf16[2,4,320,192]{3,2,1,0:T(8,128)(2,1)} %shard_map.109) | data formatting | bytes 1966080 | tf_op jit(solution)/shard_map/pallas_call | solution.py:421

commit v6 on v5

--- a/solution.py
+++ b/solution.py
@@ -20,16 +20,16 @@
 SIDES = (0, 3, 1, 2)
 TIMES = (0, 2, 1)
 ORDER = (
-    ("own", 0), ("own", 1), ("f+", 0), ("f-", 0), ("own", 2), ("f-", 1), ("g+", 1, 0), ("own", 3), ("op", 0),
-    ("query", 0), ("f+", 1), ("g+", 0, 1), ("g+", 0, 0), ("g+", 0, 3), ("g-", 1, 1), ("op", 1), ("attend", 0, 0, 1),
-    ("g-", 0, 3), ("g-", 0, 0), ("g-", 0, 1), ("f+", 2), ("g+", 3, 0), ("g-", 1, 0), ("g-", 2, 0), ("g+", 0, 2),
-    ("f-", 3), ("g-", 0, 2), ("attend", 0, 1, 2), ("table", 0), ("g-", 1, 2), ("g-", 1, 3), ("g+", 1, 1),
-    ("go", 0, 0), ("g+", 1, 3), ("f-", 2), ("g+", 1, 2), ("attend", 1, 1, 2), ("go", 0, 3), ("g+", 2, 3), ("op", 2),
-    ("go", 0, 1), ("g-", 3, 0), ("g+", 2, 0), ("f+", 3), ("go", 0, 2), ("attend", 0, 3, 2), ("op", 3), ("go", 1, 0),
-    ("g+", 3, 1), ("g-", 2, 3), ("g-", 3, 1), ("go", 1, 1), ("go", 1, 2), ("go", 1, 3), ("attend", 1, 3, 2),
-    ("g+", 2, 2), ("g+", 2, 1), ("g-", 2, 1), ("g-", 2, 2), ("attend", 2, 1, 2), ("go", 2, 0), ("g+", 3, 3),
-    ("g-", 3, 2), ("g-", 3, 3), ("g+", 3, 2), ("attend", 3, 1, 2), ("go", 3, 1), ("go", 2, 3), ("go", 2, 1),
-    ("go", 2, 2), ("attend", 2, 3, 2), ("go", 3, 3), ("go", 3, 0), ("go", 3, 2),
+    ("own", 0), ("own", 1), ("f+", 0), ("g-", 0, 0), ("f-", 0), ("own", 2), ("f-", 1), ("own", 3), ("op", 0),
+    ("g+", 1, 0), ("g-", 2, 0), ("f+", 1), ("op", 1), ("g+", 0, 1), ("g+", 0, 3), ("f+", 2), ("query", 0),
+    ("g-", 0, 3), ("g-", 0, 1), ("attend", 0, 0, 1), ("g+", 0, 0), ("g-", 1, 1), ("g-", 1, 0), ("g+", 3, 0),
+    ("g-", 0, 2), ("g+", 0, 2), ("f-", 3), ("attend", 0, 1, 2), ("table", 0), ("g+", 1, 3), ("g-", 1, 3),
+    ("g+", 1, 1), ("g-", 1, 2), ("g+", 1, 2), ("op", 2), ("attend", 1, 1, 2), ("f-", 2), ("go", 0, 0), ("go", 0, 3),
+    ("g+", 2, 0), ("g-", 3, 0), ("go", 0, 1), ("f+", 3), ("go", 0, 2), ("attend", 0, 3, 2), ("go", 1, 0), ("op", 3),
+    ("go", 1, 3), ("g-", 2, 3), ("g-", 3, 1), ("g+", 2, 3), ("go", 1, 2), ("g+", 3, 1), ("go", 1, 1),
+    ("attend", 1, 3, 2), ("g-", 2, 1), ("g+", 2, 1), ("g-", 2, 2), ("g+", 2, 2), ("attend", 2, 1, 2), ("g+", 3, 3),
+    ("g-", 3, 3), ("g-", 3, 2), ("g+", 3, 2), ("go", 3, 0), ("attend", 3, 1, 2), ("go", 2, 3), ("go", 3, 1),
+    ("go", 2, 0), ("go", 2, 1), ("go", 2, 2), ("attend", 2, 3, 2), ("go", 3, 3), ("go", 3, 2),
 )
 
 

time: 72.8 us -> 73.9 us (1.015)
  Pallas kernels: 70 us -> 70.9 us
    pallas_call x1, Pallas kernels: 70 us -> 70.9 us  [body(): pl.pallas_call(kernel, out_shape=jax.ShapeDtypeStruct((2, 4, 2 * COLS, C...]
where the time goes in v6:
time: 73.9 us; the launch traced here: 73.3 us
  Pallas kernels  70.9 us (96%)
  local copies, waits for them, and re-layouts  2.47 us (3%)
    pallas_call x1, Pallas kernels, body(): pl.pallas_call(kernel, out_shape=jax.ShapeDtypeStruct((2, 4, 2 * COLS, C...  70.9 us
    pallas_call x1, local copies, waits for them, and re-layouts, body(): pl.pallas_call(kernel, out_shape=jax.ShapeDtypeStruct((2, 4, 2 * COLS, C...  2.47 us

profile of v6, /device:TPU:1, one launch (start us, length us, event | category | flops | bytes accessed | tf_op | source)
XLA Modules:
  0.0 73.3 jit_solution(10366347510354481498)
XLA Ops:
  0.0 70.9 %shard_map.109 = bf16[2,4,320,192]{3,2,1,0:T(8,128)(2,1)} custom-call(bf16[1,2,160,384]{3,2,1,0:T(8,128)(2,1)} %latent.1, f32[384]{0:T(512)} %attn_gain_hbm.1, bf16[384,1152]{1,0:T(8,128)(2,1)} %qkv_hbm.1, bf16[384,384]{1,0:T(8,128)(2,1)} %proj_hbm.1, f32[384]{0:T(512)} %conv_gain_hbm.1, bf16[3,3,3,384,384]{4,3,2,1,0:T(8,128)(2,1)} %conv_hbm.1, ...), custom_call_target="tpu_custom_call" | custom-call | tf_op jit(solution)/shard_map/pallas_call | solution.py:421
  70.9 2.5 %copy.12 = bf16[2,4,320,192]{2,3,1,0:T(8,128)(2,1)} copy(bf16[2,4,320,192]{3,2,1,0:T(8,128)(2,1)} %shard_map.109) | data formatting | bytes 1966080 | tf_op jit(solution)/shard_map/pallas_call | solution.py:421
